TPU v7x, 32 devices: a whole 2x2x4 slice. The times are simulated.
32 devices in a mesh: rep: 4 (over z), grp: 8 (over y, x, core).
Axes of the slice: x: 2, y: 2, z: 4, core: 2. Of those that a mesh axis runs over, the one named last changes fastest.
Arguments:
- features: bfloat16 [4096, 256], P(('rep', 'grp')), may hold values from -6 to 6
- weight: bfloat16 [256, 256], replicated, may hold values from -0.375 to 0.375
- bias: float32 [256], replicated, may hold values from -3 to 3
- cotangent: bfloat16 [4096, 256], P(('rep', 'grp')), may hold values from -6 to 6
- degree: int32 [4096], P(('rep', 'grp')), may hold values from 1 to 99
- tile_cols: int32 [32, 24], P(('rep', 'grp')), may hold values from 0 to 23, as said below
- edge_tile: int32 [32, 3840], P(('rep', 'grp')), may hold values from 0 to 23
- edge_row: int32 [32, 3840], P(('rep', 'grp')), may hold values from 0 to 127
- edge_col: int32 [32, 3840], P(('rep', 'grp')), may hold values from 0 to 127
Outputs:
- hidden: bfloat16 [4096, 256], P(('rep', 'grp'))
- grad_features: bfloat16 [4096, 256], P(('rep', 'grp'))
- grad_weight: float32 [256, 256], replicated
- grad_bias: float32 [256], replicated
Inputs may be any that keep to these rules, and one draw needn't show every extreme that they name: `tile_cols`: each row lists 8 different tile columns in each of the ranges 0 to 7, 8 to 15 and 16 to 23, in that order.
All inputs are finite; a program needn't handle non-finite values.
Results may differ from a plain program's by a relative error of at most 0.0062.
Values may be sent and summed in bfloat16 or wider, within the bound.
A program may use at most 64 MiB of HBM per device.

v0:
```python
import functools

import jax
import jax.numpy as jnp
from jax import lax
from jax.experimental import pallas as pl
from jax.experimental.pallas import tpu as pltpu
from jax.sharding import PartitionSpec as P

MESH = pl.DeviceIdType.MESH
F32 = jnp.float32
BF16 = jnp.bfloat16
LIMIT = 63 * 2**20
ROWS = (((0,), (0,)), ((), ()))
LANES = (((1,), (1,)), ((), ()))


def mm(a, b, dims=(((1,), (0,)), ((), ()))):
    return lax.dot_general(a, b, dims, preferred_element_type=F32)


def kernel(
    reps,
    members,
    cols_hbm,
    features_hbm,
    weight_hbm,
    bias_hbm,
    cotangent_hbm,
    degree_hbm,
    edge_tile_hbm,
    edge_row_hbm,
    edge_col_hbm,
    hidden_hbm,
    grad_features_hbm,
    grad_weight_hbm,
    grad_bias_hbm,
    cols_ref,
    features_ref,
    weight_ref,
    bias_ref,
    cotangent_ref,
    degree_ref,
    edge_tile_ref,
    edge_row_ref,
    edge_col_ref,
    hidden_ref,
    grad_features_ref,
    grad_bias_ref,
    load_sem,
    store_sem,
    spots,
    left_hot,
    right_hot,
    listed,
    tiles_t,
    scaled,
    sums_out,
    sums,
    back,
    parts_out,
    parts,
    features_t,
    weight_out,
    weight_in,
    piece_out,
    piece_in,
    whole,
    bias_sum,
    bias_near,
    grp_send,
    grp_recv,
    rep_send,
    rep_recv,
    near_send,
    near_recv,
):
    rep = lax.axis_index("rep")
    me = lax.axis_index("grp")
    tile, width = features_ref.shape
    half = tile // 2
    edges = edge_tile_ref.shape[1]
    piece = whole.shape[1]
    chips = members // 2
    chip, core = me // 2, me % 2

    def mate(o):
        d, s = o // 2, o % 2
        return (chip + d) % chips * 2 + (core + s) % 2

    def source(o):
        d, s = o // 2, o % 2
        return (chip + chips - d) % chips * 2 + (core + s) % 2

    def reply(o):
        return (chips - o // 2) % chips * 2 + o % 2

    def peer(o):
        return (rep + o) % reps

    barrier = pltpu.get_barrier_semaphore()
    for o in range(1, members):
        pl.semaphore_signal(barrier, inc=1, device_id={"grp": mate(o)}, device_id_type=MESH)
    for o in range(1, reps):
        pl.semaphore_signal(barrier, inc=1, device_id={"rep": peer(o)}, device_id_type=MESH)
    pairs = (
        (cols_hbm, cols_ref),
        (edge_tile_hbm, edge_tile_ref),
        (edge_row_hbm, edge_row_ref),
        (edge_col_hbm, edge_col_ref),
        (features_hbm, features_ref),
        (weight_hbm, weight_ref),
        (degree_hbm, degree_ref),
        (bias_hbm, bias_ref),
        (cotangent_hbm, cotangent_ref),
    )
    loads = [
        pltpu.make_async_copy(a, b, load_sem.at[i]) for i, (a, b) in enumerate(pairs)
    ]
    for load in loads:
        load.start()

    def remote(src, dst, send, recv, to):
        return pltpu.make_async_remote_copy(
            src_ref=src,
            dst_ref=dst,
            send_sem=send,
            recv_sem=recv,
            device_id=to,
            device_id_type=MESH,
        )

    def to_mate(stage, o, src, dst):
        send, recv = grp_send.at[stage, o], grp_recv.at[stage, o]
        return remote(src, dst, send, recv, {"grp": mate(o)})

    def to_near(slot, o, src, dst):
        return remote(src, dst, near_send.at[slot], near_recv.at[slot], {"rep": peer(o)})

    def store(i, src, dst):
        copy = pltpu.make_async_copy(src, dst, store_sem.at[i])
        copy.start()
        return copy

    def begin(copies):
        for copy in copies:
            copy.start()
        return copies

    for load in loads[:4]:
        load.wait()
    edge_tile = edge_tile_ref[...]
    column = jnp.zeros_like(edge_tile)
    for t in range(cols_ref.shape[1]):
        column = jnp.where(edge_tile == t, cols_ref[0, t], column)
    listed[0, pl.ds(0, 1), :] = edge_row_ref[...]
    listed[0, pl.ds(1, 1), :] = column * tile + edge_col_ref[...]
    pl.semaphore_wait(barrier, members + reps - 2)
    edge_copies = begin(
        [to_mate(0, o, listed.at[0], listed.at[o]) for o in range(1, members)]
    )

    for load in loads[4:]:
        load.wait()
    dinv = lax.rsqrt(degree_ref[...].astype(F32))
    dinv = jnp.broadcast_to(dinv, (tile, tile)).T
    dinv = jnp.concatenate([dinv] * (width // tile), axis=1)

    own = pl.ds(tile, tile)
    scaled[own, :] = (mm(features_ref[...], weight_ref[...]) * dinv).astype(BF16)
    scaled_copies = begin(
        [
            to_near(0, 1, scaled.at[own], scaled.at[pl.ds(0, tile)]),
            to_near(1, reps - 1, scaled.at[own], scaled.at[pl.ds(2 * tile, tile)]),
        ]
    )
    features_t[...] = (
        features_ref[...].astype(F32).T.reshape(features_t.shape).astype(BF16)
    )
    spots[...] = lax.broadcasted_iota(jnp.int32, spots.shape, 0).astype(F32).astype(BF16)

    span = edges // 5 if edges % 640 == 0 else edges

    def count(o):
        row = listed[o, pl.ds(0, 1), :]
        window = listed[o, pl.ds(1, 1), :]
        column = window // tile
        part = (column >= members).astype(jnp.int32) + (column >= 2 * members).astype(jnp.int32)
        place = window - column * tile
        upper = (place >= half).astype(jnp.int32)
        left = jnp.where(column - part * members == me, upper * tile + row, -1)
        right = part * half + place - upper * half
        total = None
        for first in range(0, edges, span):
            at = pl.ds(first, span)
            for hot, key in ((left_hot, left), (right_hot, right)):
                rows = hot.shape[0]
                key = key[:, first : first + span].astype(F32)
                key = jnp.broadcast_to(key, (16, span)).astype(BF16)
                key = jnp.concatenate([key] * (rows // 16), axis=0)
                spot = jnp.concatenate([spots[:rows]] * (span // 128), axis=1)
                hot[:, at] = jnp.where(spot == key, jnp.ones_like(key), jnp.zeros_like(key))
            term = mm(right_hot[:, at], left_hot[:, at], LANES)
            total = term if total is None else total + term
        total = total.astype(BF16)
        blocks = [
            total[p * half : (p + 1) * half, u * tile : (u + 1) * tile]
            for p in range(3)
            for u in range(2)
        ]
        return jnp.concatenate(blocks, axis=0)

    counts = count(0)
    tiles_t[0] = counts
    for copy in scaled_copies:
        copy.wait_recv()
    total = mm(counts, scaled[...], ROWS)

    def sum_copy(o):
        return to_mate(1, reply(o), sums_out.at[o], sums.at[reply(o)])

    def leave(o, counts):
        sums_out[o] = mm(counts, scaled[...], ROWS).astype(BF16)
        sum_copy(o).start()

    held = None
    for o in range(1, members):
        edge_copies[o - 1].wait_recv()
        counts = count(o)
        tiles_t[o] = counts
        if held is not None:
            leave(o - 1, held)
        held = counts
    leave(members - 1, held)
    for o in range(1, members):
        to_mate(1, o, sums_out.at[o], sums.at[o]).wait_recv()
        total = total + sums[o].astype(F32)
    pre = total * dinv + bias_ref[...]
    sig = jax.nn.sigmoid(pre)
    grad_pre = cotangent_ref[...].astype(F32) * sig * (1.0 + pre * (1.0 - sig))
    back[0, pl.ds(0, tile), :] = (grad_pre * dinv).astype(BF16)
    bias_part = jnp.broadcast_to(jnp.sum(grad_pre, axis=0, keepdims=True), (8, width))
    bias_high = bias_part.astype(BF16).astype(F32)
    bias_rows = jnp.concatenate([bias_high, bias_part - bias_high], axis=0)
    back[0, pl.ds(tile, 16), :] = bias_rows.astype(BF16)
    across = [to_mate(2, o, back.at[0], back.at[o]) for o in range(2, members, 2)]
    beside = [to_mate(2, 1, back.at[0], back.at[1])]
    begin(across)
    begin(beside)
    hidden_ref[...] = (pre * sig).astype(BF16)
    stores = [store(0, hidden_ref, hidden_hbm)]

    def grad_term(o):
        return mm(tiles_t[o], back[o, pl.ds(0, tile), :])

    grads = grad_term(0)
    for d in range(1, chips):
        across[d - 1].wait_recv()
        copy = remote(
            back.at[2 * d],
            back.at[2 * d + 1],
            grp_send.at[2, 2 * d + 1],
            grp_recv.at[2, 2 * d + 1],
            {"grp": mate(1)},
        )
        copy.start()
        beside.append(copy)
        grads = grads + grad_term(2 * d)
    for d in range(chips):
        beside[d].wait_recv()
        grads = grads + grad_term(2 * d + 1)
    parts_out[pl.ds(0, tile), :] = grads[:tile].astype(BF16)
    parts_out[pl.ds(tile, tile), :] = grads[2 * tile :].astype(BF16)
    lower, upper = pl.ds(0, tile), pl.ds(tile, tile)
    part_copies = begin(
        [
            to_near(2, reps - 1, parts_out.at[lower], parts.at[lower]),
            to_near(3, 1, parts_out.at[upper], parts.at[upper]),
        ]
    )
    bias_rows = jnp.zeros((16, width), F32)
    for o in range(members):
        bias_rows = bias_rows + back[o, pl.ds(tile, 16), :].astype(F32)
    bias_total = bias_rows[:8] + bias_rows[8:]
    bias_sum[...] = bias_total
    bias_copies = begin(
        [
            remote(bias_sum, bias_near.at[o], rep_send.at[1, o], rep_recv.at[1, o], {"rep": peer(o)})
            for o in range(1, reps)
        ]
    )
    for copy in part_copies:
        copy.wait_recv()
    grad_sum = grads[tile : 2 * tile] + parts[lower, :].astype(F32) + parts[upper, :].astype(F32)
    grad_scaled = (grad_sum * dinv).astype(BF16)

    weight_copies = []
    for o in list(range(1, members)) + [0]:
        block = mm(features_t[mate(o)], grad_scaled)
        if o == 0:
            total = block
        else:
            weight_out[o] = block.astype(BF16)
            weight_copies += begin([to_mate(4, o, weight_out.at[o], weight_in.at[o])])
    grad_features_ref[...] = mm(grad_scaled, weight_ref[...], LANES).astype(BF16)
    stores.append(store(1, grad_features_ref, grad_features_hbm))
    for o, copy in enumerate(bias_copies, 1):
        copy.wait_recv()
        bias_total = bias_total + bias_near[o]
    grad_bias_ref[...] = bias_total[:1]
    stores.append(store(2, grad_bias_ref, grad_bias_hbm))
    for o, copy in enumerate(weight_copies, 1):
        copy.wait_recv()
        total = total + weight_in[o].astype(F32)
    piece_out[...] = total.astype(BF16)
    piece_copies = begin(
        [
            remote(
                piece_out, piece_in.at[o], rep_send.at[0, o], rep_recv.at[0, o], {"rep": peer(o)}
            )
            for o in range(1, reps)
        ]
    )
    for o, copy in enumerate(piece_copies, 1):
        copy.wait_recv()
    piece_in[0] = piece_out[...]
    total = piece_in[rep].astype(F32)
    for k in range(1, reps):
        total = total + piece_in[(rep - k + reps) % reps].astype(F32)
    whole[me] = total.astype(whole.dtype)
    whole_copies = begin(
        [to_mate(5, o, whole.at[me], whole.at[me]) for o in range(1, members)]
    )
    for copy in whole_copies:
        copy.wait_recv()
    stores.append(store(3, whole, grad_weight_hbm))

    for copies in (
        edge_copies,
        scaled_copies,
        bias_copies,
        across,
        beside,
        part_copies,
        weight_copies,
        piece_copies,
        whole_copies,
    ):
        for copy in copies:
            copy.wait_send()
    for o in range(1, members):
        sum_copy(o).wait_send()
    for copy in stores:
        copy.wait()


def hand_on(*refs):
    given, results, held, load_sem, store_sem = refs[:4], refs[4:8], refs[8:13], refs[13], refs[14]
    loads = [pltpu.make_async_copy(given[i], held[i], load_sem.at[i]) for i in range(4)]
    for load in loads:
        load.start()
    stores = []
    for i in (3, 0, 1, 2):
        loads[i].wait()
        source = held[i]
        if i == 2:
            source = held[4]
            source[...] = held[2][...].astype(F32).reshape(source.shape)
        stores.append(pltpu.make_async_copy(source, results[i], store_sem.at[i]))
        stores[-1].start()
    for copy in stores:
        copy.wait()


def per_device(
    reps, members, features, weight, bias, cotangent, degree, cols, edge_tile, edge_row, edge_col
):
    tile, width = features.shape
    depth = weight.shape[0]
    edges = edge_tile.shape[1]
    piece = depth // members
    args = (cols, features, weight, bias[None, :], cotangent, degree[None, :])
    args += (edge_tile, edge_row, edge_col)
    hbm = pl.BlockSpec(memory_space=pltpu.HBM)
    outs = (
        jax.ShapeDtypeStruct((tile, width), BF16),
        jax.ShapeDtypeStruct((tile, depth), BF16),
        jax.ShapeDtypeStruct((depth, width), F32),
        jax.ShapeDtypeStruct((1, width), F32),
    )
    given = outs[:2] + (jax.ShapeDtypeStruct((members, piece, width), BF16),) + outs[3:]
    results = pl.pallas_call(
        functools.partial(kernel, reps, members),
        out_shape=given,
        in_specs=[hbm] * len(args),
        out_specs=(hbm,) * 4,
        scratch_shapes=[pltpu.SMEM(cols.shape, cols.dtype)]
        + [pltpu.VMEM(a.shape, a.dtype) for a in args[1:] + outs[:2] + outs[3:]]
        + [
            pltpu.SemaphoreType.DMA((len(args),)),
            pltpu.SemaphoreType.DMA((4,)),
            pltpu.VMEM((2 * tile, 128), BF16),
            pltpu.VMEM((2 * tile, edges), BF16),
            pltpu.VMEM((3 * tile // 2, edges), BF16),
            pltpu.VMEM((members, 2, edges), jnp.int32),
            pltpu.VMEM((members, 3 * tile, tile), BF16),
            pltpu.VMEM((3 * tile, width), BF16),
            pltpu.VMEM((members, tile, width), BF16),
            pltpu.VMEM((members, tile, width), BF16),
            pltpu.VMEM((members, tile + 16, width), BF16),
            pltpu.VMEM((2 * tile, width), BF16),
            pltpu.VMEM((2 * tile, width), BF16),
            pltpu.VMEM((members, piece, tile), BF16),
            pltpu.VMEM((members, piece, width), BF16),
            pltpu.VMEM((members, piece, width), BF16),
            pltpu.VMEM((piece, width), BF16),
            pltpu.VMEM((reps, piece, width), BF16),
            pltpu.VMEM((members, piece, width), BF16),
            pltpu.VMEM((8, width), F32),
            pltpu.VMEM((reps, 8, width), F32),
            pltpu.SemaphoreType.DMA((6, members)),
            pltpu.SemaphoreType.DMA((6, members)),
            pltpu.SemaphoreType.DMA((2, reps)),
            pltpu.SemaphoreType.DMA((2, reps)),
            pltpu.SemaphoreType.DMA((4,)),
            pltpu.SemaphoreType.DMA((4,)),
        ],
        compiler_params=pltpu.CompilerParams(
            collective_id=0, has_side_effects=True, vmem_limit_bytes=LIMIT
        ),
    )(*args)
    hidden, grad_features, grad_weight, grad_bias = pl.pallas_call(
        hand_on,
        out_shape=outs,
        in_specs=[hbm] * 4,
        out_specs=(hbm,) * 4,
        scratch_shapes=[pltpu.VMEM(a.shape, a.dtype) for a in given + outs[2:3]]
        + [pltpu.SemaphoreType.DMA((4,)), pltpu.SemaphoreType.DMA((4,))],
        compiler_params=pltpu.CompilerParams(vmem_limit_bytes=LIMIT),
    )(*results)
    return hidden, grad_features, grad_weight, grad_bias[0]


def solution(mesh):
    nodes = P(("rep", "grp"), None)
    return jax.shard_map(
        functools.partial(per_device, mesh.shape["rep"], mesh.shape["grp"]),
        mesh=mesh,
        in_specs=(nodes, P(), P(), nodes, P(("rep", "grp")), nodes, nodes, nodes, nodes),
        out_specs=(nodes, nodes, P(), P()),
        check_vma=False,
    )
```

profile of v0, /device:TPU:0, one launch (start us, length us, event | category | flops | bytes accessed | tf_op | source)
XLA Modules:
  0.0 50.4 jit_solution(2497787724976505480)
XLA Ops:
  0.6 48.0 %shard_map.120 = (bf16[128,256]{1,0:T(8,128)(2,1)}, bf16[128,256]{1,0:T(8,128)(2,1)}, bf16[8,32,256]{2,1,0:T(8,128)(2,1)}, f32[1,256]{1,0:T(1,128)}) custom-call(s32[1,24]{1,0:T(1,128)} %cols_hbm.1, bf16[128,256]{1,0:T(8,128)(2,1)} %features_hbm.1, bf16[256,256]{1,0:T(8,128)(2,1)} %weight_hbm.1, f32[1,256]{1,0:T(1,128)} %bitcast.3, ...), custom_call_target="tpu_custom_call" | custom-call | tf_op jit(solution)/shard_map/pallas_call | solution.py:392
  48.7 1.8 %shard_map.121 = (bf16[128,256]{1,0:T(8,128)(2,1)}, bf16[128,256]{1,0:T(8,128)(2,1)}, f32[256,256]{1,0:T(8,128)}, f32[1,256]{1,0:T(1,128)}) custom-call(bf16[128,256]{1,0:T(8,128)(2,1)} %get-tuple-element.12.refs_0_, bf16[128,256]{1,0:T(8,128)(2,1)} %get-tuple-element.13.refs_1_, bf16[8,32,256]{2,1,0:T(8,128)(2,1)} %get-tuple-element.14.refs_2_, ...), custom_call_target="tpu_custom_call" | custom-call | tf_op jit(solution)/shard_map/pallas_call | solution.py:432
where the time goes:
time: 50.6 us; the launch traced here: 50.4 us
  Pallas kernels  49.8 us (98%)
  between operations  0.64 us (1%)
    pallas_call x1, Pallas kernels, per_device(): pl.pallas_call(functools.partial(kernel, reps, members), out_shape=given,...  48 us
    pallas_call x1, Pallas kernels, per_device(): pl.pallas_call(hand_on, out_shape=outs, in_specs=[hbm] * 4, out_specs=(hb...  1.77 us

commit v1 on v0

--- a/solution.py
+++ b/solution.py
@@ -57,6 +57,8 @@
     scaled,
     sums_out,
     sums,
+    own_sum,
+    grads,
     back,
     parts_out,
     parts,
@@ -142,6 +144,13 @@
         copy.start()
         return copy
 
+    def each(first, last, act):
+        def body(i, _):
+            act(i)
+            return 0
+
+        lax.fori_loop(first, last, body, 0)
+
     def begin(copies):
         for copy in copies:
             copy.start()
@@ -156,9 +165,11 @@
     listed[0, pl.ds(0, 1), :] = edge_row_ref[...]
     listed[0, pl.ds(1, 1), :] = column * tile + edge_col_ref[...]
     pl.semaphore_wait(barrier, members + reps - 2)
-    edge_copies = begin(
-        [to_mate(0, o, listed.at[0], listed.at[o]) for o in range(1, members)]
-    )
+
+    def edge_copy(o):
+        return to_mate(0, o, listed.at[0], listed.at[o])
+
+    each(1, members, lambda o: edge_copy(o).start())
 
     for load in loads[4:]:
         load.wait()
@@ -210,31 +221,39 @@
         ]
         return jnp.concatenate(blocks, axis=0)
 
-    counts = count(0)
-    tiles_t[0] = counts
-    for copy in scaled_copies:
-        copy.wait_recv()
-    total = mm(counts, scaled[...], ROWS)
-
     def sum_copy(o):
         return to_mate(1, reply(o), sums_out.at[o], sums.at[reply(o)])
 
-    def leave(o, counts):
-        sums_out[o] = mm(counts, scaled[...], ROWS).astype(BF16)
-        sum_copy(o).start()
-
-    held = None
-    for o in range(1, members):
-        edge_copies[o - 1].wait_recv()
-        counts = count(o)
-        tiles_t[o] = counts
-        if held is not None:
-            leave(o - 1, held)
-        held = counts
-    leave(members - 1, held)
-    for o in range(1, members):
+    def forward(o):
+        @pl.when(o > 0)
+        def _():
+            edge_copy(o).wait_recv()
+
+        tiles_t[o] = count(o)
+
+        @pl.when(o == 0)
+        def _():
+            for copy in scaled_copies:
+                copy.wait_recv()
+
+        term = mm(tiles_t[o], scaled[...], ROWS)
+
+        @pl.when(o == 0)
+        def _():
+            own_sum[...] = term
+
+        @pl.when(o > 0)
+        def _():
+            sums_out[o] = term.astype(BF16)
+            sum_copy(o).start()
+
+    each(0, members, forward)
+
+    def add_sum(o, total):
         to_mate(1, o, sums_out.at[o], sums.at[o]).wait_recv()
-        total = total + sums[o].astype(F32)
+        return total + sums[o].astype(F32)
+
+    total = lax.fori_loop(1, members, add_sum, own_sum[...])
     pre = total * dinv + bias_ref[...]
     sig = jax.nn.sigmoid(pre)
     grad_pre = cotangent_ref[...].astype(F32) * sig * (1.0 + pre * (1.0 - sig))
@@ -243,34 +262,36 @@
     bias_high = bias_part.astype(BF16).astype(F32)
     bias_rows = jnp.concatenate([bias_high, bias_part - bias_high], axis=0)
     back[0, pl.ds(tile, 16), :] = bias_rows.astype(BF16)
-    across = [to_mate(2, o, back.at[0], back.at[o]) for o in range(2, members, 2)]
-    beside = [to_mate(2, 1, back.at[0], back.at[1])]
-    begin(across)
-    begin(beside)
+    def back_copy(o):
+        return to_mate(2, o, back.at[0], back.at[o])
+
+    def relay(d):
+        send, recv = grp_send.at[2, 2 * d + 1], grp_recv.at[2, 2 * d + 1]
+        return remote(back.at[2 * d], back.at[2 * d + 1], send, recv, {"grp": mate(1)})
+
+    each(1, chips, lambda d: back_copy(2 * d).start())
+    back_copy(1).start()
     hidden_ref[...] = (pre * sig).astype(BF16)
     stores = [store(0, hidden_ref, hidden_hbm)]
 
     def grad_term(o):
         return mm(tiles_t[o], back[o, pl.ds(0, tile), :])
 
-    grads = grad_term(0)
-    for d in range(1, chips):
-        across[d - 1].wait_recv()
-        copy = remote(
-            back.at[2 * d],
-            back.at[2 * d + 1],
-            grp_send.at[2, 2 * d + 1],
-            grp_recv.at[2, 2 * d + 1],
-            {"grp": mate(1)},
-        )
-        copy.start()
-        beside.append(copy)
-        grads = grads + grad_term(2 * d)
-    for d in range(chips):
-        beside[d].wait_recv()
-        grads = grads + grad_term(2 * d + 1)
-    parts_out[pl.ds(0, tile), :] = grads[:tile].astype(BF16)
-    parts_out[pl.ds(tile, tile), :] = grads[2 * tile :].astype(BF16)
+    grads[...] = grad_term(0)
+
+    def grad_across(d):
+        back_copy(2 * d).wait_recv()
+        relay(d).start()
+        grads[...] += grad_term(2 * d)
+
+    def grad_beside(d):
+        relay(d).wait_recv()
+        grads[...] += grad_term(2 * d + 1)
+
+    each(1, chips, grad_across)
+    each(0, chips, grad_beside)
+    parts_out[pl.ds(0, tile), :] = grads[:tile, :].astype(BF16)
+    parts_out[pl.ds(tile, tile), :] = grads[2 * tile :, :].astype(BF16)
     lower, upper = pl.ds(0, tile), pl.ds(tile, tile)
     part_copies = begin(
         [
@@ -291,17 +312,18 @@
     )
     for copy in part_copies:
         copy.wait_recv()
-    grad_sum = grads[tile : 2 * tile] + parts[lower, :].astype(F32) + parts[upper, :].astype(F32)
+    grad_sum = grads[tile : 2 * tile, :] + parts[lower, :].astype(F32) + parts[upper, :].astype(F32)
     grad_scaled = (grad_sum * dinv).astype(BF16)
 
-    weight_copies = []
-    for o in list(range(1, members)) + [0]:
-        block = mm(features_t[mate(o)], grad_scaled)
-        if o == 0:
-            total = block
-        else:
-            weight_out[o] = block.astype(BF16)
-            weight_copies += begin([to_mate(4, o, weight_out.at[o], weight_in.at[o])])
+    def weight_copy(o):
+        return to_mate(3, o, weight_out.at[o], weight_in.at[o])
+
+    def weight_piece(o):
+        weight_out[o] = mm(features_t[mate(o)], grad_scaled).astype(BF16)
+        weight_copy(o).start()
+
+    each(1, members, weight_piece)
+    total = mm(features_t[me], grad_scaled)
     grad_features_ref[...] = mm(grad_scaled, weight_ref[...], LANES).astype(BF16)
     stores.append(store(1, grad_features_ref, grad_features_hbm))
     for o, copy in enumerate(bias_copies, 1):
@@ -309,9 +331,12 @@
         bias_total = bias_total + bias_near[o]
     grad_bias_ref[...] = bias_total[:1]
     stores.append(store(2, grad_bias_ref, grad_bias_hbm))
-    for o, copy in enumerate(weight_copies, 1):
-        copy.wait_recv()
-        total = total + weight_in[o].astype(F32)
+
+    def add_piece(o, total):
+        weight_copy(o).wait_recv()
+        return total + weight_in[o].astype(F32)
+
+    total = lax.fori_loop(1, members, add_piece, total)
     piece_out[...] = total.astype(BF16)
     piece_copies = begin(
         [
@@ -328,28 +353,25 @@
     for k in range(1, reps):
         total = total + piece_in[(rep - k + reps) % reps].astype(F32)
     whole[me] = total.astype(whole.dtype)
-    whole_copies = begin(
-        [to_mate(5, o, whole.at[me], whole.at[me]) for o in range(1, members)]
-    )
-    for copy in whole_copies:
-        copy.wait_recv()
+
+    def whole_copy(o):
+        return to_mate(4, o, whole.at[me], whole.at[me])
+
+    each(1, members, lambda o: whole_copy(o).start())
+    each(1, members, lambda o: whole_copy(o).wait_recv())
     stores.append(store(3, whole, grad_weight_hbm))
 
-    for copies in (
-        edge_copies,
-        scaled_copies,
-        bias_copies,
-        across,
-        beside,
-        part_copies,
-        weight_copies,
-        piece_copies,
-        whole_copies,
-    ):
+    for copies in (scaled_copies, bias_copies, part_copies, piece_copies):
         for copy in copies:
             copy.wait_send()
-    for o in range(1, members):
-        sum_copy(o).wait_send()
+
+    def sent(o):
+        for copy in (edge_copy(o), sum_copy(o), weight_copy(o), whole_copy(o)):
+            copy.wait_send()
+
+    each(1, members, sent)
+    each(1, chips, lambda d: back_copy(2 * d).wait_send())
+    each(0, chips, lambda d: relay(d).wait_send())
     for copy in stores:
         copy.wait()
 
@@ -407,6 +429,8 @@
             pltpu.VMEM((3 * tile, width), BF16),
             pltpu.VMEM((members, tile, width), BF16),
             pltpu.VMEM((members, tile, width), BF16),
+            pltpu.VMEM((tile, width), F32),
+            pltpu.VMEM((3 * tile, width), F32),
             pltpu.VMEM((members, tile + 16, width), BF16),
             pltpu.VMEM((2 * tile, width), BF16),
             pltpu.VMEM((2 * tile, width), BF16),
@@ -418,8 +442,8 @@
             pltpu.VMEM((members, piece, width), BF16),
             pltpu.VMEM((8, width), F32),
             pltpu.VMEM((reps, 8, width), F32),
-            pltpu.SemaphoreType.DMA((6, members)),
-            pltpu.SemaphoreType.DMA((6, members)),
+            pltpu.SemaphoreType.DMA((5, members)),
+            pltpu.SemaphoreType.DMA((5, members)),
             pltpu.SemaphoreType.DMA((2, reps)),
             pltpu.SemaphoreType.DMA((2, reps)),
             pltpu.SemaphoreType.DMA((4,)),

time: 50.6 us -> 48.9 us (0.966)
  Pallas kernels: 49.8 us -> 48.1 us
    pallas_call x1, Pallas kernels: 48 us -> 46.4 us  [per_device(): pl.pallas_call(functools.partial(kernel, reps, members), out_shape=given,...]
where the time goes in v1:
time: 48.9 us; the launch traced here: 48.8 us
  Pallas kernels  48.1 us (98%)
  between operations  0.64 us (1%)
    pallas_call x1, Pallas kernels, per_device(): pl.pallas_call(functools.partial(kernel, reps, members), out_shape=given,...  46.4 us
    pallas_call x1, Pallas kernels, per_device(): pl.pallas_call(hand_on, out_shape=outs, in_specs=[hbm] * 4, out_specs=(hb...  1.77 us

profile of v1, /device:TPU:0, one launch (start us, length us, event | category | flops | bytes accessed | tf_op | source)
XLA Modules:
  0.0 48.8 jit_solution(15608278539195969570)
XLA Ops:
  0.6 46.4 %shard_map.120 = (bf16[128,256]{1,0:T(8,128)(2,1)}, bf16[128,256]{1,0:T(8,128)(2,1)}, bf16[8,32,256]{2,1,0:T(8,128)(2,1)}, f32[1,256]{1,0:T(1,128)}) custom-call(s32[1,24]{1,0:T(1,128)} %cols_hbm.1, bf16[128,256]{1,0:T(8,128)(2,1)} %features_hbm.1, bf16[256,256]{1,0:T(8,128)(2,1)} %weight_hbm.1, f32[1,256]{1,0:T(1,128)} %bitcast.3, ...), custom_call_target="tpu_custom_call" | custom-call | tf_op jit(solution)/shard_map/pallas_call | solution.py:414
  47.0 1.8 %shard_map.121 = (bf16[128,256]{1,0:T(8,128)(2,1)}, bf16[128,256]{1,0:T(8,128)(2,1)}, f32[256,256]{1,0:T(8,128)}, f32[1,256]{1,0:T(1,128)}) custom-call(bf16[128,256]{1,0:T(8,128)(2,1)} %get-tuple-element.12.refs_0_, bf16[128,256]{1,0:T(8,128)(2,1)} %get-tuple-element.13.refs_1_, bf16[8,32,256]{2,1,0:T(8,128)(2,1)} %get-tuple-element.14.refs_2_, ...), custom_call_target="tpu_custom_call" | custom-call | tf_op jit(solution)/shard_map/pallas_call | solution.py:456

commit v2 on v1

--- a/solution.py
+++ b/solution.py
@@ -80,7 +80,7 @@
     rep = lax.axis_index("rep")
     me = lax.axis_index("grp")
     tile, width = features_ref.shape
-    half = tile // 2
+    middle = 3 * tile // 2
     edges = edge_tile_ref.shape[1]
     piece = whole.shape[1]
     chips = members // 2
@@ -188,7 +188,8 @@
     features_t[...] = (
         features_ref[...].astype(F32).T.reshape(features_t.shape).astype(BF16)
     )
-    spots[...] = lax.broadcasted_iota(jnp.int32, spots.shape, 0).astype(F32).astype(BF16)
+    spot = lax.broadcasted_iota(jnp.int32, spots.shape, 0) - middle
+    spots[...] = spot.astype(F32).astype(BF16)
 
     span = edges // 5 if edges % 640 == 0 else edges
 
@@ -198,28 +199,21 @@
         column = window // tile
         part = (column >= members).astype(jnp.int32) + (column >= 2 * members).astype(jnp.int32)
         place = window - column * tile
-        upper = (place >= half).astype(jnp.int32)
-        left = jnp.where(column - part * members == me, upper * tile + row, -1)
-        right = part * half + place - upper * half
+        left = jnp.where(column - part * members == me, row, -1)
+        right = part * tile + place - middle
         total = None
         for first in range(0, edges, span):
             at = pl.ds(first, span)
-            for hot, key in ((left_hot, left), (right_hot, right)):
+            for hot, key, low in ((left_hot, left, middle), (right_hot, right, 0)):
                 rows = hot.shape[0]
                 key = key[:, first : first + span].astype(F32)
                 key = jnp.broadcast_to(key, (16, span)).astype(BF16)
                 key = jnp.concatenate([key] * (rows // 16), axis=0)
-                spot = jnp.concatenate([spots[:rows]] * (span // 128), axis=1)
+                spot = jnp.concatenate([spots[low : low + rows]] * (span // 128), axis=1)
                 hot[:, at] = jnp.where(spot == key, jnp.ones_like(key), jnp.zeros_like(key))
             term = mm(right_hot[:, at], left_hot[:, at], LANES)
             total = term if total is None else total + term
-        total = total.astype(BF16)
-        blocks = [
-            total[p * half : (p + 1) * half, u * tile : (u + 1) * tile]
-            for p in range(3)
-            for u in range(2)
-        ]
-        return jnp.concatenate(blocks, axis=0)
+        return total.astype(BF16)
 
     def sum_copy(o):
         return to_mate(1, reply(o), sums_out.at[o], sums.at[reply(o)])
@@ -421,9 +415,9 @@
         + [
             pltpu.SemaphoreType.DMA((len(args),)),
             pltpu.SemaphoreType.DMA((4,)),
-            pltpu.VMEM((2 * tile, 128), BF16),
-            pltpu.VMEM((2 * tile, edges), BF16),
-            pltpu.VMEM((3 * tile // 2, edges), BF16),
+            pltpu.VMEM((3 * tile, 128), BF16),
+            pltpu.VMEM((tile, edges), BF16),
+            pltpu.VMEM((3 * tile, edges), BF16),
             pltpu.VMEM((members, 2, edges), jnp.int32),
             pltpu.VMEM((members, 3 * tile, tile), BF16),
             pltpu.VMEM((3 * tile, width), BF16),

time: 48.9 us -> 50 us (1.022)
  Pallas kernels: 48.1 us -> 49.2 us
    pallas_call x1, Pallas kernels: 46.4 us -> 47.4 us  [per_device(): pl.pallas_call(functools.partial(kernel, reps, members), out_shape=given,...]
where the time goes in v2:
time: 50 us; the launch traced here: 49.8 us
  Pallas kernels  49.2 us (98%)
  between operations  0.64 us (1%)
    pallas_call x1, Pallas kernels, per_device(): pl.pallas_call(functools.partial(kernel, reps, members), out_shape=given,...  47.4 us
    pallas_call x1, Pallas kernels, per_device(): pl.pallas_call(hand_on, out_shape=outs, in_specs=[hbm] * 4, out_specs=(hb...  1.77 us

profile of v2, /device:TPU:0, one launch (start us, length us, event | category | flops | bytes accessed | tf_op | source)
XLA Modules:
  0.0 49.8 jit_solution(15634090469426921104)
XLA Ops:
  0.6 47.4 %shard_map.120 = (bf16[128,256]{1,0:T(8,128)(2,1)}, bf16[128,256]{1,0:T(8,128)(2,1)}, bf16[8,32,256]{2,1,0:T(8,128)(2,1)}, f32[1,256]{1,0:T(1,128)}) custom-call(s32[1,24]{1,0:T(1,128)} %cols_hbm.1, bf16[128,256]{1,0:T(8,128)(2,1)} %features_hbm.1, bf16[256,256]{1,0:T(8,128)(2,1)} %weight_hbm.1, f32[1,256]{1,0:T(1,128)} %bitcast.3, ...), custom_call_target="tpu_custom_call" | custom-call | tf_op jit(solution)/shard_map/pallas_call | solution.py:408
  48.1 1.8 %shard_map.121 = (bf16[128,256]{1,0:T(8,128)(2,1)}, bf16[128,256]{1,0:T(8,128)(2,1)}, f32[256,256]{1,0:T(8,128)}, f32[1,256]{1,0:T(1,128)}) custom-call(bf16[128,256]{1,0:T(8,128)(2,1)} %get-tuple-element.12.refs_0_, bf16[128,256]{1,0:T(8,128)(2,1)} %get-tuple-element.13.refs_1_, bf16[8,32,256]{2,1,0:T(8,128)(2,1)} %get-tuple-element.14.refs_2_, ...), custom_call_target="tpu_custom_call" | custom-call | tf_op jit(solution)/shard_map/pallas_call | solution.py:450

commit v3 on v1

--- a/solution.py
+++ b/solution.py
@@ -10,6 +10,7 @@
 MESH = pl.DeviceIdType.MESH
 F32 = jnp.float32
 BF16 = jnp.bfloat16
+F8 = jnp.float8_e4m3fn
 LIMIT = 63 * 2**20
 ROWS = (((0,), (0,)), ((), ()))
 LANES = (((1,), (1,)), ((), ()))
@@ -210,7 +211,8 @@
                 key = jnp.broadcast_to(key, (16, span)).astype(BF16)
                 key = jnp.concatenate([key] * (rows // 16), axis=0)
                 spot = jnp.concatenate([spots[:rows]] * (span // 128), axis=1)
-                hot[:, at] = jnp.where(spot == key, jnp.ones_like(key), jnp.zeros_like(key))
+                hit = jnp.where(spot == key, jnp.ones_like(key), jnp.zeros_like(key))
+                hot[:, at] = hit.astype(hot.dtype)
             term = mm(right_hot[:, at], left_hot[:, at], LANES)
             total = term if total is None else total + term
         total = total.astype(BF16)
@@ -422,8 +424,8 @@
             pltpu.SemaphoreType.DMA((len(args),)),
             pltpu.SemaphoreType.DMA((4,)),
             pltpu.VMEM((2 * tile, 128), BF16),
-            pltpu.VMEM((2 * tile, edges), BF16),
-            pltpu.VMEM((3 * tile // 2, edges), BF16),
+            pltpu.VMEM((2 * tile, edges), F8),
+            pltpu.VMEM((3 * tile // 2, edges), F8),
             pltpu.VMEM((members, 2, edges), jnp.int32),
             pltpu.VMEM((members, 3 * tile, tile), BF16),
             pltpu.VMEM((3 * tile, width), BF16),

time: 48.9 us -> 47.6 us (0.973)
  Pallas kernels: 48.1 us -> 46.8 us
    pallas_call x1, Pallas kernels: 46.4 us -> 45.1 us  [per_device(): pl.pallas_call(functools.partial(kernel, reps, members), out_shape=given,...]
where the time goes in v3:
time: 47.6 us; the launch traced here: 47.5 us
  Pallas kernels  46.8 us (98%)
  between operations  0.64 us (1%)
    pallas_call x1, Pallas kernels, per_device(): pl.pallas_call(functools.partial(kernel, reps, members), out_shape=given,...  45.1 us
    pallas_call x1, Pallas kernels, per_device(): pl.pallas_call(hand_on, out_shape=outs, in_specs=[hbm] * 4, out_specs=(hb...  1.77 us

profile of v3, /device:TPU:0, one launch (start us, length us, event | category | flops | bytes accessed | tf_op | source)
XLA Modules:
  0.0 47.5 jit_solution(5859408976931903331)
XLA Ops:
  0.6 45.1 %shard_map.120 = (bf16[128,256]{1,0:T(8,128)(2,1)}, bf16[128,256]{1,0:T(8,128)(2,1)}, bf16[8,32,256]{2,1,0:T(8,128)(2,1)}, f32[1,256]{1,0:T(1,128)}) custom-call(s32[1,24]{1,0:T(1,128)} %cols_hbm.1, bf16[128,256]{1,0:T(8,128)(2,1)} %features_hbm.1, bf16[256,256]{1,0:T(8,128)(2,1)} %weight_hbm.1, f32[1,256]{1,0:T(1,128)} %bitcast.3, ...), custom_call_target="tpu_custom_call" | custom-call | tf_op jit(solution)/shard_map/pallas_call | solution.py:416
  45.7 1.8 %shard_map.121 = (bf16[128,256]{1,0:T(8,128)(2,1)}, bf16[128,256]{1,0:T(8,128)(2,1)}, f32[256,256]{1,0:T(8,128)}, f32[1,256]{1,0:T(1,128)}) custom-call(bf16[128,256]{1,0:T(8,128)(2,1)} %get-tuple-element.12.refs_0_, bf16[128,256]{1,0:T(8,128)(2,1)} %get-tuple-element.13.refs_1_, bf16[8,32,256]{2,1,0:T(8,128)(2,1)} %get-tuple-element.14.refs_2_, ...), custom_call_target="tpu_custom_call" | custom-call | tf_op jit(solution)/shard_map/pallas_call | solution.py:458
